TPU v7x, 256 devices: a whole 4x4x8 slice. The times are simulated.
256 devices in a mesh: row: 16 (over z_hi, x), col: 16 (over z_lo, y, core).
Axes of the slice: x: 4, y: 4, z: 8 (z_hi: 4, z_lo: 2; z = z_hi * 2 + z_lo), core: 2. Of those that a mesh axis runs over, the one named last changes fastest.
Arguments:
- blocks: bfloat16 [48, 896, 896], P('row', 'col'), may hold values from -0.4375 to 0.4375
- eps_occ: float32 [192], P('row'), may hold values from -2 to -0.4
- eps_vir: float32 [224], replicated, may hold values from 0.2 to 2.5
- pairs: int32 [512, 2], P('row'), may hold values from -1 to 47, as said below
Outputs:
- gradient: float32 [48, 896, 896], P('row', 'col')
Inputs may be any that keep to these rules, and one draw needn't show every extreme that they name: `pairs`: slot s belongs to row group g = s // 32. A live slot holds two block ids (first, second): first is one of the 3 blocks g * 3 to g * 3 + 2; second is a block of group g not smaller than first, or a block of group g + 1 (mod 16). No pair appears twice. A dead slot holds -1 in both entries. Each row group has exactly 12 live slots.
All inputs are finite; a program needn't handle non-finite values.
Results may differ from a plain program's by a relative error of at most 0.002.
Values may be sent and summed in bfloat16 or wider, within the bound.
A program may use at most 128 MiB of HBM per device.

v0:
```python
import jax
import jax.numpy as jnp
from jax import lax
from jax.sharding import PartitionSpec as P


def from_behind(shard, axis, by):
    size = lax.axis_size(axis)
    return lax.ppermute(shard, axis, [(i, (i + by) % size) for i in range(size)])


def pair_terms(left_matrix, right_matrix, first_energy, second_energy, eps_vir):
    orbitals = first_energy.shape[0]
    virtuals = eps_vir.shape[0]
    width = orbitals * virtuals
    integrals = lax.dot_general(
        left_matrix, right_matrix, (((0,), (0,)), ((), ())), preferred_element_type=jnp.float32
    )
    gaps = (
        first_energy[:, None, None, None]
        + second_energy[None, None, :, None]
        - eps_vir[None, :, None, None]
        - eps_vir[None, None, None, :]
    )
    amplitude = integrals.reshape(orbitals, virtuals, orbitals, virtuals) / gaps
    combined = (
        (2.0 * amplitude - jnp.transpose(amplitude, (0, 3, 2, 1)))
        .astype(jnp.bfloat16)
        .reshape(width, width)
    )
    first_grad = lax.dot_general(
        right_matrix, combined, (((1,), (1,)), ((), ())), preferred_element_type=jnp.float32
    )
    second_grad = jnp.dot(left_matrix, combined, preferred_element_type=jnp.float32)
    return (first_grad, second_grad)


def add_block(totals, update, position):
    current = lax.dynamic_index_in_dim(totals, position, 0, keepdims=False)
    return lax.dynamic_update_index_in_dim(totals, current + update, position, 0)


def body(blocks, eps_occ, eps_vir, pairs):
    group_size, aux_slice, width = blocks.shape
    orbitals = eps_occ.shape[0] // group_size
    row_count = lax.axis_size("row")
    col_count = lax.axis_size("col")
    total_blocks = group_size * row_count
    first_block = lax.axis_index("row") * group_size
    column = lax.axis_index("col")
    next_blocks, next_energy = (
        from_behind(blocks, "row", -1),
        from_behind(eps_occ.astype(jnp.bfloat16), "row", -1).astype(eps_occ.dtype),
    )
    extended = jnp.concatenate([blocks, next_blocks], 0)
    extended_energy = jnp.concatenate([eps_occ, next_energy], 0)
    live = pairs[:, 0] >= 0
    local_ids = jnp.where(live[:, None], (pairs - first_block) % total_blocks, 0)
    slot_total = pairs.shape[0]
    per_device = slot_total // col_count

    def energies(position):
        return lax.dynamic_slice_in_dim(extended_energy, position * orbitals, orbitals)

    whole = lax.all_gather(extended, "col", axis=1, tiled=True)
    picked = lax.dynamic_slice_in_dim(local_ids, column * per_device, per_device, 0)
    usable = lax.dynamic_slice_in_dim(live, column * per_device, per_device, 0)
    picked, usable = (picked, usable)
    totals = jnp.zeros(whole.shape, jnp.float32)
    for number in range(per_device):
        first_pos = picked[number, 0]
        second_pos = picked[number, 1]

        def work(current):
            first_rows = lax.dynamic_index_in_dim(whole, first_pos, 0, keepdims=False)
            second_rows = lax.dynamic_index_in_dim(whole, second_pos, 0, keepdims=False)
            first_grad, second_grad = pair_terms(
                first_rows, second_rows, energies(first_pos), energies(second_pos), eps_vir
            )
            current = add_block(current, first_grad, first_pos)
            return add_block(current, second_grad, second_pos)

        def skip(current):
            return current

        totals = lax.cond(usable[number], work, skip, totals)
    summed = lax.psum_scatter(totals, "col", scatter_dimension=1, tiled=True)
    from_next = from_behind(summed[group_size:], "row", 1)
    return summed[:group_size] + from_next


def solution(mesh):
    in_specs = (P("row", "col", None), P("row"), P(), P("row", None))
    out_specs = P("row", "col", None)
    return jax.shard_map(body, mesh=mesh, in_specs=in_specs, out_specs=out_specs, check_vma=False)
```

profile of v0, /device:TPU:1, one launch (start us, length us, event | category | flops | bytes accessed | tf_op | source)
XLA Modules:
  0.0 361.9 jit_solution(16872984676219312451)
XLA Ops:
  6.5 0.0 all-gather.2.cloned.1.call-start
  6.5 9.0 %collective-permute-start = (bf16[3,56,896]{2,1,0:T(8,128)(2,1)}, bf16[3,56,896]{2,1,0:T(8,128)(2,1)S(1)}, u32[]{:S(2)}, u32[]{:S(2)}) collective-permute-start(bf16[3,56,896]{2,1,0:T(8,128)(2,1)} %param.8), channel_id=1, source_target_pairs={{0,240},{16,0},{32,16},{48,32},{64,48},{80,64},{96,80},{112,96},{1... | collective-permute-start | bytes 903176 | tf_op jit(solution)/shard_map/ppermute | solution.py:9
  15.6 10.1 %collective-permute-done = bf16[3,56,896]{2,1,0:T(8,128)(2,1)S(1)} collective-permute-done((bf16[3,56,896]{2,1,0:T(8,128)(2,1)}, bf16[3,56,896]{2,1,0:T(8,128)(2,1)S(1)}, u32[]{:S(2)}, u32[]{:S(2)}) %collective-permute-start) | collective-permute-done | bytes 301088 | tf_op jit(solution)/shard_map/ppermute | solution.py:9
  25.7 1.8 pad_maximum_fusion
  27.5 0.0 all-gather.2.cloned.1.call-update
  27.6 0.0 reduce-scatter.2.cloned.1.call-start
  27.6 0.7 convert_element_type.30
  28.3 8.9 %collective-permute-start.1 = (bf16[12]{0:T(256)(128)(2,1)S(1)}, bf16[12]{0:T(256)(128)(2,1)S(1)}, u32[]{:S(2)}, u32[]{:S(2)}) collective-permute-start(bf16[12]{0:T(256)(128)(2,1)S(1)} %convert_element_type.30), channel_id=1, source_target_pairs={{0,240},{16,0},{32,16},{48,32},{64,48},{80,64},{96,80},{112,96},{1... | collective-permute-start | bytes 80 | tf_op jit(solution)/shard_map/ppermute | solution.py:9
  37.1 0.7 fusion.9
  37.8 0.1 constant_dynamic-slice_fusion.8
  37.9 0.7 fusion.13
  39.9 0.7 fusion.8
  40.6 0.1 constant_dynamic-slice_fusion.7
  40.7 0.0 collective-permute-done.1
  40.7 0.7 pad_maximum_fusion.1
  41.4 50.6 %all-gather.2.cloned.1.call-done = bf16[6,896,896]{2,1,0:T(8,128)(2,1)} async-done(((bf16[6,56,896]{2,1,0:T(8,128)(2,1)}), bf16[6,896,896]{2,1,0:T(8,128)(2,1)}) %all-gather.2.cloned.1.call-update) | async-done | bytes 9633808 | tf_op jit(solution)/shard_map/all_gather | solution.py:65
  92.0 7.8 %conditional.2 = (f32[6,896,896]{2,1,0:T(8,128)}) conditional(s32[]{:T(128)} %bitcast.32, () %tuple.17, (s32[2,2]{0,1:T(2,128)S(1)}, bf16[6,896,896]{2,1,0:T(8,128)(2,1)}, s32[2,2]{0,1:T(2,128)S(1)}, f32[24]{0:T(128)S(1)}, f32[224]{0:T(256)}) %tuple.18), branch_computations={%region_0.1_spmd, %region_1.2_spmd} | conditional | flops 4322368512 | bytes 107641608 | solution.py:86
  92.0 7.8 %broadcast_in_dim.32 = f32[6,896,896]{2,1,0:T(8,128)} broadcast(f32[]{:T(128)} %constant.61.clone), dimensions={} | broadcast | bytes 19267588 | tf_op jit(solution)/shard_map/broadcast_in_dim | solution.py:69
  99.9 0.0 reduce-scatter.2.cloned.1.call-update
  99.9 226.1 %reduce-scatter.2.cloned.1.call-done = f32[6,56,896]{2,1,0:T(8,128)} async-done(((f32[6,896,896]{2,1,0:T(8,128)}), f32[6,56,896]{2,1,0:T(8,128)}) %reduce-scatter.2.cloned.1.call-update) | async-done | bytes 1204240 | tf_op jit(solution)/shard_map/reduce_scatter | solution.py:87
  326.0 1.1 slice.41
  327.1 1.3 collective-permute-start.2
  328.4 24.8 %collective-permute-done.2 = f32[3,56,896]{2,1,0:T(8,128)S(1)} collective-permute-done((f32[3,56,896]{2,1,0:T(8,128)S(1)}, f32[3,56,896]{2,1,0:T(8,128)S(1)}, u32[]{:S(2)}, u32[]{:S(2)}) %collective-permute-start.2) | collective-permute-done | bytes 602144 | tf_op jit(solution)/shard_map/ppermute | solution.py:9
  353.2 1.9 slice_add_fusion
  (2 shorter events, 0.0 us)
Async XLA Ops:
  6.5 85.5 %all-gather.2.cloned.1.call-start = ((), (), s32[]{:S(2)}) async-start(), calls=%async_computation.1 | async-start | bytes 10235904 | tf_op jit(solution)/shard_map/all_gather | solution.py:65
  6.5 19.1 %collective-permute-start = (bf16[3,56,896]{2,1,0:T(8,128)(2,1)}, bf16[3,56,896]{2,1,0:T(8,128)(2,1)S(1)}, u32[]{:S(2)}, u32[]{:S(2)}) collective-permute-start(bf16[3,56,896]{2,1,0:T(8,128)(2,1)} %param.8), channel_id=1, source_target_pairs={{0,240},{16,0},{32,16},{48,32},{64,48},{80,64},{96,80},{112,96},{1... | collective-permute-start | bytes 903176 | tf_op jit(solution)/shard_map/ppermute | solution.py:9
  27.6 298.4 %reduce-scatter.2.cloned.1.call-start = ((), (), s32[]{:S(2)}) async-start(), calls=%async_computation.2 | async-start | bytes 20471808 | tf_op jit(solution)/shard_map/reduce_scatter | solution.py:87
  28.3 12.4 %collective-permute-start.1 = (bf16[12]{0:T(256)(128)(2,1)S(1)}, bf16[12]{0:T(256)(128)(2,1)S(1)}, u32[]{:S(2)}, u32[]{:S(2)}) collective-permute-start(bf16[12]{0:T(256)(128)(2,1)S(1)} %convert_element_type.30), channel_id=1, source_target_pairs={{0,240},{16,0},{32,16},{48,32},{64,48},{80,64},{96,80},{112,96},{1... | collective-permute-start | bytes 80 | tf_op jit(solution)/shard_map/ppermute | solution.py:9
  327.1 26.1 %collective-permute-start.2 = (f32[3,56,896]{2,1,0:T(8,128)S(1)}, f32[3,56,896]{2,1,0:T(8,128)S(1)}, u32[]{:S(2)}, u32[]{:S(2)}) collective-permute-start(f32[3,56,896]{2,1,0:T(8,128)S(1)} %slice.41), channel_id=1, source_target_pairs={{0,16},{16,32},{32,48},{48,64},{64,80},{80,96},{96,112},{112,128},... | collective-permute-start | bytes 1806344 | tf_op jit(solution)/shard_map/ppermute | solution.py:9
Sparse Core Ops, SparseCore 0:
  27.7 64.3 all-gather.1
  100.0 225.9 reduce-scatter.1
where the time goes:
time: 369 us; the launch traced here: 362 us
  waiting for transfers between devices  312 us (85%)
  starting transfers between devices  19.2 us (5%)
  between operations  14.8 us (4%)
  local copies, waits for them, and re-layouts  9.76 us (3%)
  other arithmetic  6.56 us (2%)
    reduce_scatter x1, waiting for transfers between devices, body(): summed = lax.psum_scatter(totals, 'col', scatter_dimension=1, tiled=True)  226 us
    all_gather x1, waiting for transfers between devices, body(): whole = lax.all_gather(extended, 'col', axis=1, tiled=True)  50.6 us
    ppermute x3, waiting for transfers between devices, from_behind(): lax.ppermute(shard, axis, [(i, (i + by) % size) for i in range(size)])  34.9 us
    ppermute x3, starting transfers between devices, from_behind(): lax.ppermute(shard, axis, [(i, (i + by) % size) for i in range(size)])  19.2 us
    broadcast_in_dim x1, local copies, waits for them, and re-layouts, body(): totals = jnp.zeros(whole.shape, jnp.float32)  7.84 us
  transfers between devices with their start and end apart: 5, of which 4 were waited for; matrix products, arithmetic and copies ran while one was open for 1% of the time, Pallas kernels for 0%

commit v1 on v0

v1 whole, which is shorter than its diff:
```python
import functools

import jax
import jax.numpy as jnp
from jax import lax
from jax.experimental import pallas as pl
from jax.experimental.pallas import tpu as pltpu
from jax.sharding import PartitionSpec as P

NONE = 7
OWN = (3, 4, 3, 4, 3, 4, 2, NONE, 0, 1, 5, 1, 1, 2, 0, 1)
SHARED = (0, 1, 2, NONE, 5, 2, 0, NONE)
COLS = 16
CHIPS = 8
ROWS = 56
SLOT = 64
ORB = 4
VIRT = 224
PAD = 256
WIDTH = ORB * VIRT
WIDE = ORB * PAD
FULL = COLS * SLOT
MESH = pl.DeviceIdType.MESH


def packed(table):
    return sum(value << (3 * place) for place, value in enumerate(table))


def own_of(c):
    low, high = packed(OWN[:8]), packed(OWN[8:])
    return (jnp.where(c < 8, low, high) >> (3 * (c % 8))) & 7


def shared_of(q):
    return (jnp.int32(packed(SHARED)) >> (3 * q)) & 7


def away(c, t):
    z, y, k = c // 8, (c // 2) % 4, c % 2
    dz, dy, dk = t // 8, (t // 2) % 4, t % 2
    return ((z + dz) % 2) * 8 + ((y + dy) % 4) * 2 + (k + dk) % 2


def kernel(
    blocks, eps, vir, pairs, out,
    nxt, energy, own_slots, shared_slots, y_wide, u_mat, ut_mat, gaps, alive,
    g_own, g_keep, g_give, g_sib, g_sum, r_own, r_shared, give_back, got_back,
    nxt_sem, own_send, own_recv, shared_send, shared_recv, hand_send,
    sib_send, sib_recv, term_send, term_recv, sum_send, sum_recv, back_send, back_recv,
):
    row = lax.axis_index("row")
    c = lax.axis_index("col")
    n_row = lax.axis_size("row")
    ahead, behind = (row + 1) % n_row, (row + n_row - 1) % n_row
    q, k = c // 2, c % 2
    sibling = q * 2 + 1 - k
    mine, common = own_of(c), shared_of(q)
    paired = common != NONE

    barrier = pltpu.get_barrier_semaphore()

    def greet(t, _):
        pl.semaphore_signal(barrier, inc=1, device_id={"col": away(c, t)}, device_id_type=MESH)
        return 0

    lax.fori_loop(1, COLS, greet, 0)
    for r in (ahead, behind):
        pl.semaphore_signal(barrier, inc=1, device_id={"row": r}, device_id_type=MESH)
    pl.semaphore_wait(barrier, COLS - 1 + 2)

    def remote(src, dst, send, recv, where):
        return pltpu.make_async_remote_copy(
            src_ref=src, dst_ref=dst, send_sem=send, recv_sem=recv, device_id=where, device_id_type=MESH
        )

    ship = remote(blocks, nxt, nxt_sem.at[0], nxt_sem.at[1], {"row": behind})
    ship_energy = remote(eps, energy.at[pl.ds(3, 3)], nxt_sem.at[2], nxt_sem.at[3], {"row": behind})
    ship.start()
    ship_energy.start()

    def own_copy(source, t, target, index):
        return remote(source.at[index], own_slots.at[c], own_send.at[t], own_recv.at[c], {"col": target})

    def shared_copy(source, t, target, index):
        return remote(source.at[index], shared_slots.at[c], shared_send.at[t], shared_recv.at[c], {"col": target})

    def send_blocks(source, first):
        def step(t, _):
            target = away(c, t)
            block = own_of(target)

            @pl.when((t > 0) & (block >= first) & (block < first + 3))
            def _():
                own_copy(source, t, target, block - first).start()

            block2 = shared_of(target // 2)

            @pl.when((t > 0) & (t % 2 == 0) & (block2 >= first) & (block2 < first + 3))
            def _():
                shared_copy(source, t // 2, target, block2 - first).start()

            return 0

        lax.fori_loop(0, COLS, step, 0)

        @pl.when((mine >= first) & (mine < first + 3))
        def _():
            own_slots[c] = source[mine - first]

        @pl.when((common >= first) & (common < first + 3))
        def _():
            shared_slots[c] = source[common - first]

    send_blocks(blocks, 0)

    y_wide[...] = jnp.zeros_like(y_wide)
    energy[pl.ds(0, 3)] = eps[...]
    virtual = jnp.broadcast_to(vir[...], (PAD, PAD))
    gaps[...] = virtual + virtual.T
    low, high = jnp.minimum(mine, common), jnp.where(common == NONE, mine, jnp.maximum(mine, common))
    first_id = row * 3 + low
    second_id = (row * 3 + high) % (n_row * 3)
    listed = pairs[...]
    hit = (listed[:, 0:1] == first_id) & (listed[:, 1:2] == second_id)
    alive[...] = jnp.broadcast_to(jnp.sum(jnp.where(hit, 1.0, 0.0), axis=0, keepdims=True), (8, 128))

    ship.wait_recv()
    send_blocks(nxt, 3)
    ship_energy.wait_recv()

    def unpack(which, slots, source):
        value = slots[source]
        at = pl.ds(pl.multiple_of(source * SLOT, SLOT), ROWS)
        for i in range(ORB):
            y_wide[which, at, pl.ds(i * PAD, VIRT)] = value[:, i * VIRT : (i + 1) * VIRT]

    def hand(source):
        return remote(
            shared_slots.at[source], shared_slots.at[source], hand_send.at[source // 2], shared_recv.at[source],
            {"col": sibling},
        )

    @pl.when(paired)
    def _():
        def step(t, _):
            source = away(c, 2 * t)

            @pl.when(t > 0)
            def _():
                hand(source).wait_recv()

            hand(source).start()
            unpack(1, shared_slots, source)
            return 0

        lax.fori_loop(0, CHIPS, step, 0)

    @pl.when(mine != NONE)
    def _():
        unpack(0, own_slots, c)

        def step(t, _):
            source = away(c, t)
            remote(blocks.at[0], own_slots.at[source], own_send.at[t], own_recv.at[source], {"col": source}).wait_recv()
            unpack(0, own_slots, source)
            return 0

        lax.fori_loop(1, COLS, step, 0)

    @pl.when(paired)
    def _():
        def step(t, _):
            source = away(sibling, 2 * t)
            hand(source).wait_recv()
            unpack(1, shared_slots, source)
            return 0

        lax.fori_loop(0, CHIPS, step, 0)

    partner = jnp.where(paired, 1, 0)
    mine_index = jnp.where(mine == NONE, 0, mine)
    common_index = jnp.where(paired, common, mine_index)

    def amplitudes(i, _):
        left = y_wide[0, :, pl.ds(pl.multiple_of(i * PAD, PAD), PAD)]
        at = pl.ds(pl.multiple_of(i * VIRT, 32), VIRT)
        energy_i = energy[mine_index, pl.ds(i, 1), :]
        energy_i = jnp.concatenate([energy_i, energy_i], axis=1)
        live = alive[0:1, 0:1]
        for j in range(ORB):
            right = y_wide[partner, :, j * PAD : (j + 1) * PAD]
            integrals = lax.dot_general(left, right, (((0,), (0,)), ((), ())), preferred_element_type=jnp.float32)
            energy_j = energy[common_index, j : j + 1, :]
            energy_j = jnp.concatenate([energy_j, energy_j], axis=1)
            amplitude = live * integrals / ((energy_i + energy_j) - gaps[...])
            flipped = amplitude.T
            u_mat[at, j * PAD : (j + 1) * PAD] = (2.0 * amplitude - flipped)[:VIRT].astype(jnp.bfloat16)
            ut_mat[j * VIRT : (j + 1) * VIRT, pl.ds(pl.multiple_of(i * PAD, PAD), PAD)] = (
                (2.0 * flipped - amplitude)[:VIRT].astype(jnp.bfloat16)
            )
        return 0

    lax.fori_loop(0, ORB, amplitudes, 0)

    def term_copy(target):
        return remote(g_own.at[target], r_own.at[c], term_send.at[target], term_recv.at[c], {"col": target})

    def sib_copy(chip):
        return remote(g_give.at[chip], g_sib.at[chip], sib_send.at[chip], sib_recv.at[chip], {"col": sibling})

    def sum_copy(chip):
        return remote(g_sum.at[chip], r_shared.at[q], sum_send.at[chip], sum_recv.at[q], {"col": chip * 2 + k})

    def part_of(step):
        return (c // 4 + 1 + step) % 4

    def add_shared(step):
        for h in range(2):
            chip = part_of(step) * 2 + h
            sib_copy(chip).wait_recv()
            total = (g_keep[chip] + g_sib[chip].astype(jnp.float32)).astype(jnp.bfloat16)
            g_sum[chip] = total

            @pl.when(chip != q)
            def _():
                sum_copy(chip).start()

            @pl.when(chip == q)
            def _():
                r_shared[q] = total

    def terms(step, _):
        part = part_of(step)
        at = pl.ds(pl.multiple_of(part * PAD, PAD), PAD)
        dims = (((1,), (1,)), ((), ()))
        to_shared = lax.dot_general(y_wide[0, at, :], ut_mat[...], dims, preferred_element_type=jnp.float32)

        @pl.when(paired)
        def _():
            for h in range(2):
                chip = part * 2 + h
                even = to_shared[2 * h * SLOT : 2 * h * SLOT + ROWS]
                odd = to_shared[(2 * h + 1) * SLOT : (2 * h + 1) * SLOT + ROWS]
                g_keep[chip] = jnp.where(k == 0, even, odd)
                g_give[chip] = jnp.where(k == 0, odd, even).astype(jnp.bfloat16)
                sib_copy(chip).start()

        to_own = lax.dot_general(y_wide[partner, at, :], u_mat[...], dims, preferred_element_type=jnp.float32)
        to_own = to_own + jnp.where(paired, 0.0, 1.0) * to_shared
        for n in range(4):
            target = part * 4 + n
            value = to_own[n * SLOT : n * SLOT + ROWS].astype(jnp.bfloat16)
            g_own[target] = value

            @pl.when((target != c) & (mine != NONE))
            def _():
                term_copy(target).start()

            @pl.when(target == c)
            def _():
                r_own[c] = value

        @pl.when(paired & (step > 0))
        def _():
            add_shared(step - 1)

        return 0

    lax.fori_loop(0, 4, terms, 0)

    @pl.when(paired)
    def _():
        add_shared(3)

    def total_of(block):
        total = jnp.zeros((ROWS, WIDTH), jnp.float32)
        for source in range(COLS):
            if OWN[source] == block:
                @pl.when(c != source)
                def _():
                    remote(
                        g_own.at[0], r_own.at[source], term_send.at[0], term_recv.at[source], {"col": sibling}
                    ).wait_recv()

                total = total + r_own[source].astype(jnp.float32)
        for chip in range(CHIPS):
            if SHARED[chip] == block:
                @pl.when(q != chip)
                def _():
                    remote(
                        g_sum.at[0], r_shared.at[chip], sum_send.at[0], sum_recv.at[chip], {"col": sibling}
                    ).wait_recv()

                total = total + r_shared[chip].astype(jnp.float32)
        return total

    def back_copy(index):
        return remote(
            give_back.at[index], got_back.at[index], back_send.at[index], back_recv.at[index], {"row": ahead}
        )

    for index in range(3):
        give_back[index] = total_of(3 + index).astype(jnp.bfloat16)
        back_copy(index).start()
    for index in range(3):
        total = total_of(index)
        back_copy(index).wait_recv()
        out[index] = total + got_back[index].astype(jnp.float32)

    ship.wait_send()
    ship_energy.wait_send()
    for index in range(3):
        back_copy(index).wait_send()

    def drain(t, _):
        target = away(c, t)

        @pl.when((t > 0) & (own_of(target) != NONE))
        def _():
            own_copy(blocks, t, target, 0).wait_send()

        @pl.when((t > 0) & (t % 2 == 0) & (shared_of(target // 2) != NONE))
        def _():
            shared_copy(blocks, t // 2, target, 0).wait_send()

        @pl.when((t > 0) & (mine != NONE))
        def _():
            term_copy(target).wait_send()

        return 0

    lax.fori_loop(0, COLS, drain, 0)

    @pl.when(paired)
    def _():
        def drain_chip(t, _):
            hand(away(c, 2 * t)).wait_send()
            sib_copy(t).wait_send()

            @pl.when(t != q)
            def _():
                sum_copy(t).wait_send()

            return 0

        lax.fori_loop(0, CHIPS, drain_chip, 0)


def body(blocks, eps_occ, eps_vir, pairs):
    eps = jnp.broadcast_to(eps_occ.reshape(3, ORB, 1), (3, ORB, 128))
    vir = jnp.pad(eps_vir, (0, PAD - VIRT)).reshape(1, PAD)
    vmem = pl.BlockSpec(memory_space=pltpu.VMEM)
    bf16, f32 = jnp.bfloat16, jnp.float32
    dma = pltpu.SemaphoreType.DMA
    slab = (ROWS, WIDTH)
    return pl.pallas_call(
        kernel,
        out_shape=jax.ShapeDtypeStruct(blocks.shape, f32),
        in_specs=[vmem] * 4,
        out_specs=vmem,
        scratch_shapes=[
            pltpu.VMEM((3,) + slab, bf16),
            pltpu.VMEM((6, ORB, 128), f32),
            pltpu.VMEM((COLS,) + slab, bf16),
            pltpu.VMEM((COLS,) + slab, bf16),
            pltpu.VMEM((2, FULL, WIDE), bf16),
            pltpu.VMEM((WIDTH, WIDE), bf16),
            pltpu.VMEM((WIDTH, WIDE), bf16),
            pltpu.VMEM((PAD, PAD), f32),
            pltpu.VMEM((8, 128), f32),
            pltpu.VMEM((COLS,) + slab, bf16),
            pltpu.VMEM((CHIPS,) + slab, f32),
            pltpu.VMEM((CHIPS,) + slab, bf16),
            pltpu.VMEM((CHIPS,) + slab, bf16),
            pltpu.VMEM((CHIPS,) + slab, bf16),
            pltpu.VMEM((COLS,) + slab, bf16),
            pltpu.VMEM((CHIPS,) + slab, bf16),
            pltpu.VMEM((3,) + slab, bf16),
            pltpu.VMEM((3,) + slab, bf16),
            dma((4,)),
            dma((COLS,)), dma((COLS,)), dma((CHIPS,)), dma((COLS,)), dma((CHIPS,)),
            dma((CHIPS,)), dma((CHIPS,)), dma((COLS,)), dma((COLS,)), dma((CHIPS,)), dma((CHIPS,)),
            dma((3,)), dma((3,)),
        ],
        compiler_params=pltpu.CompilerParams(
            collective_id=0, has_side_effects=True, vmem_limit_bytes=48 * 1024 * 1024
        ),
        cost_estimate=pl.CostEstimate(flops=6 * FULL**3, bytes_accessed=4 * 1024 * 1024, transcendentals=0),
    )(blocks, eps, vir, pairs)


def solution(mesh):
    in_specs = (P("row", "col", None), P("row"), P(), P("row", None))
    out_specs = P("row", "col", None)
    return jax.shard_map(body, mesh=mesh, in_specs=in_specs, out_specs=out_specs, check_vma=False)
```

time: 369 us -> 105 us (0.28); the launches traced: 362 us -> 104 us
  waiting for transfers between devices: 312 us -> 0 us
  Pallas kernels: 0 us -> 100 us
  starting transfers between devices: 19.2 us -> 0 us
  between operations: 14.8 us -> 0.01 us
  other arithmetic: 6.56 us -> 0 us
  local copies, waits for them, and re-layouts: 9.76 us -> 3.97 us
    reduce_scatter x1 -> x0, waiting for transfers between devices: 226 us -> none  [body(): summed = lax.psum_scatter(totals, 'col', scatter_dimension=1, tiled=True)]
    pallas_call x0 -> x1, Pallas kernels: none -> 100 us  [body(): pl.pallas_call(kernel, out_shape=jax.ShapeDtypeStruct(blocks.shape, f32),...]
    all_gather x1 -> x0, waiting for transfers between devices: 50.6 us -> none  [body(): whole = lax.all_gather(extended, 'col', axis=1, tiled=True)]
    ppermute x3 -> x0, waiting for transfers between devices: 34.9 us -> none  [from_behind(): lax.ppermute(shard, axis, [(i, (i + by) % size) for i in range(size)])]
    ppermute x3 -> x0, starting transfers between devices: 19.2 us -> none  [from_behind(): lax.ppermute(shard, axis, [(i, (i + by) % size) for i in range(size)])]
    broadcast_in_dim x1 -> x2, local copies, waits for them, and re-layouts: 7.84 us -> 0.15 us  [body(): eps = jnp.broadcast_to(eps_occ.reshape(3, ORB, 1), (3, ORB, 128))]
  transfers between devices with their start and end apart: 5 -> 0, of which waited for: 4 -> 0; matrix products, arithmetic and copies ran while one was open for 1% -> 0% of each run, Pallas kernels for 0% -> 0%
where the time goes in v1:
time: 105 us; the launch traced here: 104 us
  Pallas kernels  100 us (95%)
  local copies, waits for them, and re-layouts  3.97 us (4%)
    pallas_call x1, Pallas kernels, body(): pl.pallas_call(kernel, out_shape=jax.ShapeDtypeStruct(blocks.shape, f32),...  100 us
    unnamed x8, local copies, waits for them, and re-layouts  3.13 us

profile of v1, /device:TPU:1, one launch (start us, length us, event | category | flops | bytes accessed | tf_op | source)
XLA Modules:
  0.0 104.4 jit_solution(15901560127603600658)
XLA Ops:
  0.0 0.7 pad.4
  0.7 0.0 copy-start.2
  0.7 0.7 copy-done.2
  1.3 0.1 broadcast_in_dim.7
  1.4 0.0 copy-start.1
  1.4 0.1 broadcast_in_dim.8.eps
  1.5 0.6 copy-done.1
  2.1 0.1 copy.5.pairs
  2.2 0.0 copy-start
  2.2 1.0 copy-done
  3.2 100.4 %shard_map.46 = f32[3,56,896]{2,1,0:T(8,128)S(1)} custom-call(bf16[3,56,896]{2,1,0:T(8,128)(2,1)S(1)} %copy-done, f32[3,4,128]{2,1,0:T(4,128)S(1)} %broadcast_in_dim.8.eps, f32[1,256]{1,0:T(1,128)S(1)} %bitcast.1, s32[32,2]{1,0:T(8,128)S(1)} %copy.5.pairs), custom_call_target="tpu_custom_call" | custom-call | flops 6442450944 | bytes 4194304 | tf_op jit(solution)/shard_map/pallas_call | solution.py:357
  103.6 0.8 copy.7
Async XLA Ops:
  0.7 0.7 copy-start.2
  1.4 0.7 copy-start.1
  2.2 1.0 copy-start

commit v2 on v1

v2 whole, which is shorter than its diff:
```python
import functools

import jax
import jax.numpy as jnp
from jax import lax
from jax.experimental import pallas as pl
from jax.experimental.pallas import tpu as pltpu
from jax.sharding import PartitionSpec as P

NONE = 7
OWN = (0, 1, 5, 1, 1, 2, 0, 1, 3, 4, 3, 4, 3, 4, 2, NONE)
SHARED = (5, 2, 0, NONE, 0, 1, 2, NONE)
NEXT = ((5,), (3, 4))
PLANE = 8
RING = 4
COLS = 16
CHIPS = 8
ROWS = 56
SLOT = 64
ORB = 4
VIRT = 224
PAD = 256
WIDTH = ORB * VIRT
WIDE = ORB * PAD
FULL = COLS * SLOT
MESH = pl.DeviceIdType.MESH


def packed(table):
    return sum(value << (3 * place) for place, value in enumerate(table))


def own_of(c):
    low, high = packed(OWN[:8]), packed(OWN[8:])
    return (jnp.where(c < 8, low, high) >> (3 * (c % 8))) & 7


def shared_of(q):
    return (jnp.int32(packed(SHARED)) >> (3 * q)) & 7


def kernel(
    blocks, eps, vir, pairs, out,
    across, nxt, energy, own_slots, shared_slots, y_wide, u_mat, ut_mat, gaps, alive,
    g_own, g_keep, g_give, g_sib, g_sum, r_own, r_shared, give_back, got_back, give_across, got_across,
    energy_sem, across_send, across_recv, next_send, next_recv,
    own_send, own_recv, shared_send, shared_recv, hand_send,
    sib_send, sib_recv, term_send, term_recv, sum_send, sum_recv, back_send, back_recv, cross_send, cross_recv,
):
    row = lax.axis_index("row")
    c = lax.axis_index("col")
    n_row = lax.axis_size("row")
    ahead, behind = (row + 1) % n_row, (row + n_row - 1) % n_row
    z, y, k = c // PLANE, (c // 2) % RING, c % 2
    q, here = c // 2, c % PLANE
    sibling = q * 2 + 1 - k
    partner_z = (1 - z) * PLANE + here
    mine, common = own_of(c), shared_of(q)
    paired = common != NONE

    def place(t):
        return ((y + t // 2) % RING) * 2 + (k + t % 2) % 2

    barrier = pltpu.get_barrier_semaphore()

    def greet(t, _):
        pl.semaphore_signal(barrier, inc=1, device_id={"col": z * PLANE + place(t)}, device_id_type=MESH)
        return 0

    for r in (behind, ahead):
        for half in range(2):
            pl.semaphore_signal(
                barrier, inc=1, device_id={"row": r, "col": half * PLANE + here}, device_id_type=MESH
            )
    pl.semaphore_signal(barrier, inc=1, device_id={"col": partner_z}, device_id_type=MESH)
    lax.fori_loop(1, PLANE, greet, 0)
    pl.semaphore_wait(barrier, PLANE - 1 + 1 + 4)

    def remote(src, dst, send, recv, where):
        return pltpu.make_async_remote_copy(
            src_ref=src, dst_ref=dst, send_sem=send, recv_sem=recv, device_id=where, device_id_type=MESH
        )

    def ship(index, half, source_half):
        return remote(
            blocks.at[index], nxt.at[source_half, index], next_send.at[index], next_recv.at[source_half * 3 + index],
            {"row": behind, "col": half * PLANE + here},
        )

    def cross(index):
        return remote(
            blocks.at[index], across.at[index], across_send.at[index], across_recv.at[index], {"col": partner_z}
        )

    ship_energy = remote(eps, energy.at[pl.ds(3, 3)], energy_sem.at[0], energy_sem.at[1], {"row": behind})
    for half in (1, 0):
        for block in NEXT[half]:
            ship(block - 3, half, z).start()
    for index in range(3):
        cross(index).start()
    ship_energy.start()

    def own_copy(source, far, t, index):
        slot = ((z + far) % 2) * PLANE + here
        return remote(
            source.at[index], own_slots.at[slot], own_send.at[far * PLANE + t], own_recv.at[slot],
            {"col": z * PLANE + place(t)},
        )

    def shared_copy(source, far, t, index):
        slot = ((z + far) % 2) * PLANE + here
        return remote(
            source.at[index], shared_slots.at[slot], shared_send.at[far * RING + t // 2], shared_recv.at[slot],
            {"col": z * PLANE + place(t)},
        )

    def send_blocks(source, far, first):
        def step(t, _):
            target = z * PLANE + place(t)
            block = own_of(target)

            @pl.when((block >= first) & (block < first + 3))
            def _():
                own_copy(source, far, t, block - first).start()

            block2 = shared_of(target // 2)

            @pl.when((t % 2 == 0) & (block2 >= first) & (block2 < first + 3))
            def _():
                shared_copy(source, far, t, block2 - first).start()

            return 0

        lax.fori_loop(1, PLANE, step, 0)
        slot = ((z + far) % 2) * PLANE + here

        @pl.when((mine >= first) & (mine < first + 3))
        def _():
            own_slots[slot] = source[mine - first]

        @pl.when((common >= first) & (common < first + 3))
        def _():
            shared_slots[slot] = source[common - first]

    send_blocks(blocks, 0, 0)

    y_wide[...] = jnp.zeros_like(y_wide)
    energy[pl.ds(0, 3)] = eps[...]
    virtual = jnp.broadcast_to(vir[...], (PAD, PAD))
    gaps[...] = virtual + virtual.T
    low, high = jnp.minimum(mine, common), jnp.where(common == NONE, mine, jnp.maximum(mine, common))
    first_id = row * 3 + low
    second_id = (row * 3 + high) % (n_row * 3)
    listed = pairs[...]
    hit = (listed[:, 0:1] == first_id) & (listed[:, 1:2] == second_id)
    alive[...] = jnp.broadcast_to(jnp.sum(jnp.where(hit, 1.0, 0.0), axis=0, keepdims=True), (8, 128))

    for index in range(3):
        cross(index).wait_recv()
    send_blocks(across, 1, 0)

    for far in range(2):
        source_half = (z + far) % 2
        for half in range(2):
            @pl.when(z == half)
            def _():
                for block in NEXT[half]:
                    ship(block - 3, half, source_half).wait_recv()

        send_blocks(nxt.at[source_half], far, 3)
    ship_energy.wait_recv()

    def unpack(which, slots, source):
        value = slots[source]
        at = pl.ds(pl.multiple_of(source * SLOT, SLOT), ROWS)
        for i in range(ORB):
            y_wide[which, at, pl.ds(i * PAD, VIRT)] = value[:, i * VIRT : (i + 1) * VIRT]

    def hand(source):
        return remote(
            shared_slots.at[source], shared_slots.at[source], hand_send.at[source // 2], shared_recv.at[source],
            {"col": sibling},
        )

    @pl.when(paired)
    def _():
        def step(t, _):
            source = ((z + t // RING) % 2) * PLANE + ((y + t) % RING) * 2 + k

            @pl.when(t % RING > 0)
            def _():
                hand(source).wait_recv()

            hand(source).start()
            unpack(1, shared_slots, source)
            return 0

        lax.fori_loop(0, CHIPS, step, 0)

    @pl.when(mine != NONE)
    def _():
        def step(t, _):
            source = ((z + t // PLANE) % 2) * PLANE + place(t % PLANE)

            @pl.when(t % PLANE > 0)
            def _():
                remote(
                    blocks.at[0], own_slots.at[source], own_send.at[t], own_recv.at[source], {"col": sibling}
                ).wait_recv()

            unpack(0, own_slots, source)
            return 0

        lax.fori_loop(0, COLS, step, 0)

    @pl.when(paired)
    def _():
        def step(t, _):
            source = ((z + t // RING) % 2) * PLANE + ((y + t) % RING) * 2 + 1 - k
            hand(source).wait_recv()
            unpack(1, shared_slots, source)
            return 0

        lax.fori_loop(0, CHIPS, step, 0)

    partner = jnp.where(paired, 1, 0)
    mine_index = jnp.where(mine == NONE, 0, mine)
    common_index = jnp.where(paired, common, mine_index)

    def amplitudes(i, _):
        left = y_wide[0, :, pl.ds(pl.multiple_of(i * PAD, PAD), PAD)]
        at = pl.ds(pl.multiple_of(i * VIRT, 32), VIRT)
        energy_i = energy[mine_index, pl.ds(i, 1), :]
        energy_i = jnp.concatenate([energy_i, energy_i], axis=1)
        live = alive[0:1, 0:1]
        for j in range(ORB):
            right = y_wide[partner, :, j * PAD : (j + 1) * PAD]
            integrals = lax.dot_general(left, right, (((0,), (0,)), ((), ())), preferred_element_type=jnp.float32)
            energy_j = energy[common_index, j : j + 1, :]
            energy_j = jnp.concatenate([energy_j, energy_j], axis=1)
            amplitude = live * integrals / ((energy_i + energy_j) - gaps[...])
            flipped = amplitude.T
            u_mat[at, j * PAD : (j + 1) * PAD] = (2.0 * amplitude - flipped)[:VIRT].astype(jnp.bfloat16)
            ut_mat[j * VIRT : (j + 1) * VIRT, pl.ds(pl.multiple_of(i * PAD, PAD), PAD)] = (
                (2.0 * flipped - amplitude)[:VIRT].astype(jnp.bfloat16)
            )
        return 0

    lax.fori_loop(0, ORB, amplitudes, 0)

    def term_copy(s):
        return remote(
            g_own.at[s], r_own.at[(s // PLANE) * PLANE + here], term_send.at[s],
            term_recv.at[(s // PLANE) * PLANE + here], {"col": z * PLANE + s % PLANE},
        )

    def sib_copy(chip):
        return remote(g_give.at[chip], g_sib.at[chip], sib_send.at[chip], sib_recv.at[chip], {"col": sibling})

    def sum_copy(chip):
        at = (chip // RING) * RING + y
        return remote(
            g_sum.at[chip], r_shared.at[at], sum_send.at[chip], sum_recv.at[at],
            {"col": z * PLANE + (chip % RING) * 2 + k},
        )

    def part_of(step):
        return ((z + 1 + step // 2) % 2) * 2 + (y // 2 + 1 + step) % 2

    def add_shared(step):
        for h in range(2):
            chip = part_of(step) * 2 + h
            sib_copy(chip).wait_recv()
            total = (g_keep[chip] + g_sib[chip].astype(jnp.float32)).astype(jnp.bfloat16)
            g_sum[chip] = total

            @pl.when(chip % RING != y)
            def _():
                sum_copy(chip).start()

            @pl.when(chip % RING == y)
            def _():
                r_shared[chip] = total

    def terms(step, _):
        part = part_of(step)
        at = pl.ds(pl.multiple_of(part * PAD, PAD), PAD)
        dims = (((1,), (1,)), ((), ()))
        to_shared = lax.dot_general(y_wide[0, at, :], ut_mat[...], dims, preferred_element_type=jnp.float32)

        @pl.when(paired)
        def _():
            for h in range(2):
                chip = part * 2 + h
                even = to_shared[2 * h * SLOT : 2 * h * SLOT + ROWS]
                odd = to_shared[(2 * h + 1) * SLOT : (2 * h + 1) * SLOT + ROWS]
                g_keep[chip] = jnp.where(k == 0, even, odd)
                g_give[chip] = jnp.where(k == 0, odd, even).astype(jnp.bfloat16)
                sib_copy(chip).start()

        to_own = lax.dot_general(y_wide[partner, at, :], u_mat[...], dims, preferred_element_type=jnp.float32)
        to_own = to_own + jnp.where(paired, 0.0, 1.0) * to_shared
        for n in range(4):
            target = part * 4 + n
            value = to_own[n * SLOT : n * SLOT + ROWS].astype(jnp.bfloat16)
            g_own[target] = value

            @pl.when((target % PLANE != here) & (mine != NONE))
            def _():
                term_copy(target).start()

            @pl.when(target % PLANE == here)
            def _():
                r_own[target] = value

        @pl.when(paired & (step > 0))
        def _():
            add_shared(step - 1)

        return 0

    lax.fori_loop(0, 4, terms, 0)

    @pl.when(paired)
    def _():
        add_shared(3)

    def total_of(half, at, block):
        total = jnp.zeros((ROWS, WIDTH), jnp.float32)
        for source in range(PLANE):
            if OWN[half * PLANE + source] == block:
                @pl.when(here != source)
                def _():
                    remote(
                        g_own.at[0], r_own.at[at * PLANE + source], term_send.at[0],
                        term_recv.at[at * PLANE + source], {"col": sibling},
                    ).wait_recv()

                total = total + r_own[at * PLANE + source].astype(jnp.float32)
        for chip in range(RING):
            if SHARED[half * RING + chip] == block:
                @pl.when(y != chip)
                def _():
                    remote(
                        g_sum.at[0], r_shared.at[at * RING + chip], sum_send.at[0],
                        sum_recv.at[at * RING + chip], {"col": sibling},
                    ).wait_recv()

                total = total + r_shared[at * RING + chip].astype(jnp.float32)
        return total

    def back_copy(index, at):
        return remote(
            give_back.at[at, index], got_back.at[index], back_send.at[at * 3 + index], back_recv.at[index],
            {"row": ahead, "col": at * PLANE + here},
        )

    def cross_copy(index):
        return remote(
            give_across.at[index], got_across.at[index], cross_send.at[index], cross_recv.at[index],
            {"col": partner_z},
        )

    for half in range(2):
        @pl.when(z == half)
        def _():
            for at in (1 - half, half):
                for block in NEXT[half]:
                    give_back[at, block - 3] = total_of(half, at, block).astype(jnp.bfloat16)
                    back_copy(block - 3, at).start()
                for index in range(3):
                    total = total_of(half, at, index)
                    if at == half:
                        out[index] = total
                    else:
                        give_across[index] = total.astype(jnp.bfloat16)
                        cross_copy(index).start()

    for index in range(3):
        cross_copy(index).wait_recv()
        back_copy(index, 0).wait_recv()
        out[index] += got_across[index].astype(jnp.float32) + got_back[index].astype(jnp.float32)

    ship_energy.wait_send()
    for index in range(3):
        cross(index).wait_send()
        ship(index, 0, 0).wait_send()
        cross_copy(index).wait_send()
    for half in range(2):
        @pl.when(z == half)
        def _():
            for at in range(2):
                for block in NEXT[half]:
                    back_copy(block - 3, at).wait_send()

    def drain(n, _):
        far, t = n // PLANE, n % PLANE
        target = z * PLANE + place(t)

        @pl.when((t > 0) & (own_of(target) != NONE))
        def _():
            own_copy(blocks, far, t, 0).wait_send()

        @pl.when((t > 0) & (t % 2 == 0) & (shared_of(target // 2) != NONE))
        def _():
            shared_copy(blocks, far, t, 0).wait_send()

        @pl.when((n % PLANE != here) & (mine != NONE))
        def _():
            term_copy(n).wait_send()

        return 0

    lax.fori_loop(0, COLS, drain, 0)

    @pl.when(paired)
    def _():
        def drain_chip(chip, _):
            hand(chip * 2 + k).wait_send()
            sib_copy(chip).wait_send()

            @pl.when(chip % RING != y)
            def _():
                sum_copy(chip).wait_send()

            return 0

        lax.fori_loop(0, CHIPS, drain_chip, 0)


def body(blocks, eps_occ, eps_vir, pairs):
    eps = jnp.broadcast_to(eps_occ.reshape(3, ORB, 1), (3, ORB, 128))
    vir = jnp.pad(eps_vir, (0, PAD - VIRT)).reshape(1, PAD)
    vmem = pl.BlockSpec(memory_space=pltpu.VMEM)
    bf16, f32 = jnp.bfloat16, jnp.float32
    dma = pltpu.SemaphoreType.DMA
    slab = (ROWS, WIDTH)
    return pl.pallas_call(
        kernel,
        out_shape=jax.ShapeDtypeStruct(blocks.shape, f32),
        in_specs=[vmem] * 4,
        out_specs=vmem,
        scratch_shapes=[
            pltpu.VMEM((3,) + slab, bf16),
            pltpu.VMEM((2, 3) + slab, bf16),
            pltpu.VMEM((6, ORB, 128), f32),
            pltpu.VMEM((COLS,) + slab, bf16),
            pltpu.VMEM((COLS,) + slab, bf16),
            pltpu.VMEM((2, FULL, WIDE), bf16),
            pltpu.VMEM((WIDTH, WIDE), bf16),
            pltpu.VMEM((WIDTH, WIDE), bf16),
            pltpu.VMEM((PAD, PAD), f32),
            pltpu.VMEM((8, 128), f32),
            pltpu.VMEM((COLS,) + slab, bf16),
            pltpu.VMEM((CHIPS,) + slab, f32),
            pltpu.VMEM((CHIPS,) + slab, bf16),
            pltpu.VMEM((CHIPS,) + slab, bf16),
            pltpu.VMEM((CHIPS,) + slab, bf16),
            pltpu.VMEM((COLS,) + slab, bf16),
            pltpu.VMEM((CHIPS,) + slab, bf16),
            pltpu.VMEM((2, 3) + slab, bf16),
            pltpu.VMEM((3,) + slab, bf16),
            pltpu.VMEM((3,) + slab, bf16),
            pltpu.VMEM((3,) + slab, bf16),
            dma((2,)), dma((3,)), dma((3,)), dma((3,)), dma((6,)),
            dma((COLS,)), dma((COLS,)), dma((CHIPS,)), dma((COLS,)), dma((CHIPS,)),
            dma((CHIPS,)), dma((CHIPS,)), dma((COLS,)), dma((COLS,)), dma((CHIPS,)), dma((CHIPS,)),
            dma((6,)), dma((3,)), dma((3,)), dma((3,)),
        ],
        compiler_params=pltpu.CompilerParams(
            collective_id=0, has_side_effects=True, vmem_limit_bytes=48 * 1024 * 1024
        ),
        cost_estimate=pl.CostEstimate(flops=6 * FULL**3, bytes_accessed=4 * 1024 * 1024, transcendentals=0),
    )(blocks, eps, vir, pairs)


def solution(mesh):
    in_specs = (P("row", "col", None), P("row"), P(), P("row", None))
    out_specs = P("row", "col", None)
    return jax.shard_map(body, mesh=mesh, in_specs=in_specs, out_specs=out_specs, check_vma=False)
```

time: 105 us -> 92.9 us (0.88)
  the two profiles are of different devices: /device:TPU:1 before, /device:TPU:10 now
where the time goes in v2:
time: 92.9 us; the launch traced here: 92.7 us
  Pallas kernels  88.7 us (95%)
  local copies, waits for them, and re-layouts  3.97 us (4%)
    pallas_call x1, Pallas kernels, body(): pl.pallas_call(kernel, out_shape=jax.ShapeDtypeStruct(blocks.shape, f32),...  88.7 us
    unnamed x8, local copies, waits for them, and re-layouts  3.13 us

profile of v2, /device:TPU:10, one launch (start us, length us, event | category | flops | bytes accessed | tf_op | source)
XLA Modules:
  0.0 92.7 jit_solution(10260674945724834525)
XLA Ops:
  0.0 0.7 pad.4
  0.7 0.0 copy-start.2
  0.7 0.7 copy-done.2
  1.3 0.1 broadcast_in_dim.7
  1.4 0.0 copy-start.1
  1.4 0.1 broadcast_in_dim.8.eps
  1.5 0.6 copy-done.1
  2.1 0.1 copy.5.pairs
  2.2 0.0 copy-start
  2.2 1.0 %copy-done = bf16[3,56,896]{2,1,0:T(8,128)(2,1)S(1)} copy-done((bf16[3,56,896]{2,1,0:T(8,128)(2,1)S(1)}, bf16[3,56,896]{2,1,0:T(8,128)(2,1)}, u32[]{:S(2)}) %copy-start) | copy-done | bytes 301080
  3.2 88.7 %shard_map.46 = f32[3,56,896]{2,1,0:T(8,128)S(1)} custom-call(bf16[3,56,896]{2,1,0:T(8,128)(2,1)S(1)} %copy-done, f32[3,4,128]{2,1,0:T(4,128)S(1)} %broadcast_in_dim.8.eps, f32[1,256]{1,0:T(1,128)S(1)} %bitcast.1, s32[32,2]{1,0:T(8,128)S(1)} %copy.5.pairs), custom_call_target="tpu_custom_call" | custom-call | flops 6442450944 | bytes 4194304 | tf_op jit(solution)/shard_map/pallas_call | solution.py:438
  91.9 0.8 copy.7
Async XLA Ops:
  0.7 0.7 copy-start.2
  1.4 0.7 copy-start.1
  2.2 1.0 %copy-start = (bf16[3,56,896]{2,1,0:T(8,128)(2,1)S(1)}, bf16[3,56,896]{2,1,0:T(8,128)(2,1)}, u32[]{:S(2)}) copy-start(bf16[3,56,896]{2,1,0:T(8,128)(2,1)} %blocks.1) | copy-start | bytes 903172

commit v3 on v2

--- a/solution.py
+++ b/solution.py
@@ -8,8 +8,8 @@
 from jax.sharding import PartitionSpec as P
 
 NONE = 7
-OWN = (0, 1, 5, 1, 1, 2, 0, 1, 3, 4, 3, 4, 3, 4, 2, NONE)
-SHARED = (5, 2, 0, NONE, 0, 1, 2, NONE)
+OWN = (0, 1, 1, 2, 5, 1, 0, 1, 0, 1, 0, 1, 3, 4, 2, NONE)
+SHARED = (5, 0, 2, NONE, 3, 4, 2, NONE)
 NEXT = ((5,), (3, 4))
 PLANE = 8
 RING = 4
@@ -40,8 +40,9 @@
 
 
 def kernel(
-    blocks, eps, vir, pairs, out,
-    across, nxt, energy, own_slots, shared_slots, y_wide, u_mat, ut_mat, gaps, alive,
+    blocks_in, eps_in, vir_in, pairs_in, out,
+    blocks, levels, vir, pairs, fetch_sem,
+    across, nxt, energy, virtual_row, own_slots, shared_slots, y_wide, u_mat, ut_mat, gaps, alive,
     g_own, g_keep, g_give, g_sib, g_sum, r_own, r_shared, give_back, got_back, give_across, got_across,
     energy_sem, across_send, across_recv, next_send, next_recv,
     own_send, own_recv, shared_send, shared_recv, hand_send,
@@ -61,6 +62,14 @@
     def place(t):
         return ((y + t // 2) % RING) * 2 + (k + t % 2) % 2
 
+    fetches = [
+        pltpu.make_async_copy(source, target, fetch_sem.at[n])
+        for n, (source, target) in enumerate(
+            ((blocks_in, blocks), (eps_in, levels.at[0]), (vir_in, vir), (pairs_in, pairs))
+        )
+    ]
+    for fetch in fetches:
+        fetch.start()
     barrier = pltpu.get_barrier_semaphore()
 
     def greet(t, _):
@@ -75,6 +84,8 @@
     pl.semaphore_signal(barrier, inc=1, device_id={"col": partner_z}, device_id_type=MESH)
     lax.fori_loop(1, PLANE, greet, 0)
     pl.semaphore_wait(barrier, PLANE - 1 + 1 + 4)
+    for fetch in fetches:
+        fetch.wait()
 
     def remote(src, dst, send, recv, where):
         return pltpu.make_async_remote_copy(
@@ -92,12 +103,12 @@
             blocks.at[index], across.at[index], across_send.at[index], across_recv.at[index], {"col": partner_z}
         )
 
-    ship_energy = remote(eps, energy.at[pl.ds(3, 3)], energy_sem.at[0], energy_sem.at[1], {"row": behind})
+    ship_energy = remote(levels.at[0], levels.at[1], energy_sem.at[0], energy_sem.at[1], {"row": behind})
+    for index in range(3):
+        cross(index).start()
     for half in (1, 0):
         for block in NEXT[half]:
             ship(block - 3, half, z).start()
-    for index in range(3):
-        cross(index).start()
     ship_energy.start()
 
     def own_copy(source, far, t, index):
@@ -145,15 +156,15 @@
     send_blocks(blocks, 0, 0)
 
     y_wide[...] = jnp.zeros_like(y_wide)
-    energy[pl.ds(0, 3)] = eps[...]
-    virtual = jnp.broadcast_to(vir[...], (PAD, PAD))
+    virtual_row[...] = jnp.zeros_like(virtual_row)
+    virtual_row[:, 0:VIRT] = vir[...]
+    virtual = jnp.broadcast_to(virtual_row[...], (PAD, PAD))
     gaps[...] = virtual + virtual.T
     low, high = jnp.minimum(mine, common), jnp.where(common == NONE, mine, jnp.maximum(mine, common))
     first_id = row * 3 + low
     second_id = (row * 3 + high) % (n_row * 3)
-    listed = pairs[...]
-    hit = (listed[:, 0:1] == first_id) & (listed[:, 1:2] == second_id)
-    alive[...] = jnp.broadcast_to(jnp.sum(jnp.where(hit, 1.0, 0.0), axis=0, keepdims=True), (8, 128))
+    hit = (pairs[0:1, :] == first_id) & (pairs[1:2, :] == second_id)
+    alive[...] = jnp.broadcast_to(jnp.sum(jnp.where(hit, 1.0, 0.0), axis=1, keepdims=True), (8, 128))
 
     for index in range(3):
         cross(index).wait_recv()
@@ -226,18 +237,22 @@
     partner = jnp.where(paired, 1, 0)
     mine_index = jnp.where(mine == NONE, 0, mine)
     common_index = jnp.where(paired, common, mine_index)
+    lane = lax.broadcasted_iota(jnp.int32, (1, 3 * ORB), 1)
+    for which, index in enumerate((mine_index, common_index)):
+        held = levels[index // 3]
+        for i in range(ORB):
+            level = jnp.sum(jnp.where(lane == (index % 3) * ORB + i, held, 0.0), axis=1, keepdims=True)
+            energy[which, i : i + 1, :] = jnp.broadcast_to(level, (1, PAD))
 
     def amplitudes(i, _):
         left = y_wide[0, :, pl.ds(pl.multiple_of(i * PAD, PAD), PAD)]
         at = pl.ds(pl.multiple_of(i * VIRT, 32), VIRT)
-        energy_i = energy[mine_index, pl.ds(i, 1), :]
-        energy_i = jnp.concatenate([energy_i, energy_i], axis=1)
+        energy_i = energy[0, pl.ds(i, 1), :]
         live = alive[0:1, 0:1]
         for j in range(ORB):
             right = y_wide[partner, :, j * PAD : (j + 1) * PAD]
             integrals = lax.dot_general(left, right, (((0,), (0,)), ((), ())), preferred_element_type=jnp.float32)
-            energy_j = energy[common_index, j : j + 1, :]
-            energy_j = jnp.concatenate([energy_j, energy_j], axis=1)
+            energy_j = energy[1, j : j + 1, :]
             amplitude = live * integrals / ((energy_i + energy_j) - gaps[...])
             flipped = amplitude.T
             u_mat[at, j * PAD : (j + 1) * PAD] = (2.0 * amplitude - flipped)[:VIRT].astype(jnp.bfloat16)
@@ -282,46 +297,60 @@
             def _():
                 r_shared[chip] = total
 
-    def terms(step, _):
+    def product(which, at, matrix):
+        dims = (((1,), (1,)), ((), ()))
+        return lax.dot_general(y_wide[which, at, :], matrix[...], dims, preferred_element_type=jnp.float32)
+
+    def send_terms(part, values):
+        for n in range(4):
+            target = part * 4 + n
+            value = values[n * SLOT : n * SLOT + ROWS].astype(jnp.bfloat16)
+            g_own[target] = value
+
+            @pl.when(target % PLANE != here)
+            def _():
+                term_copy(target).start()
+
+            @pl.when(target % PLANE == here)
+            def _():
+                r_own[target] = value
+
+    shared_start = jnp.where(common >= 3, 0, 4)
+
+    def terms(turn, _):
+        step = turn % 4
         part = part_of(step)
         at = pl.ds(pl.multiple_of(part * PAD, PAD), PAD)
-        dims = (((1,), (1,)), ((), ()))
-        to_shared = lax.dot_general(y_wide[0, at, :], ut_mat[...], dims, preferred_element_type=jnp.float32)
-
-        @pl.when(paired)
-        def _():
+        shared_turn = turn // 4 == shared_start // 4
+
+        @pl.when(paired & shared_turn)
+        def _():
+            values = product(0, at, ut_mat)
             for h in range(2):
                 chip = part * 2 + h
-                even = to_shared[2 * h * SLOT : 2 * h * SLOT + ROWS]
-                odd = to_shared[(2 * h + 1) * SLOT : (2 * h + 1) * SLOT + ROWS]
+                even = values[2 * h * SLOT : 2 * h * SLOT + ROWS]
+                odd = values[(2 * h + 1) * SLOT : (2 * h + 1) * SLOT + ROWS]
                 g_keep[chip] = jnp.where(k == 0, even, odd)
                 g_give[chip] = jnp.where(k == 0, odd, even).astype(jnp.bfloat16)
                 sib_copy(chip).start()
 
-        to_own = lax.dot_general(y_wide[partner, at, :], u_mat[...], dims, preferred_element_type=jnp.float32)
-        to_own = to_own + jnp.where(paired, 0.0, 1.0) * to_shared
-        for n in range(4):
-            target = part * 4 + n
-            value = to_own[n * SLOT : n * SLOT + ROWS].astype(jnp.bfloat16)
-            g_own[target] = value
-
-            @pl.when((target % PLANE != here) & (mine != NONE))
-            def _():
-                term_copy(target).start()
-
-            @pl.when(target % PLANE == here)
-            def _():
-                r_own[target] = value
-
-        @pl.when(paired & (step > 0))
-        def _():
-            add_shared(step - 1)
+        @pl.when(paired & jnp.logical_not(shared_turn))
+        def _():
+            send_terms(part, product(1, at, u_mat))
+
+        @pl.when(jnp.logical_not(paired) & (mine != NONE) & (turn < 4))
+        def _():
+            send_terms(part, product(0, at, u_mat) + product(0, at, ut_mat))
+
+        @pl.when(paired & (turn > shared_start) & (turn <= shared_start + 4))
+        def _():
+            add_shared(turn - shared_start - 1)
 
         return 0
 
-    lax.fori_loop(0, 4, terms, 0)
-
-    @pl.when(paired)
+    lax.fori_loop(0, 8, terms, 0)
+
+    @pl.when(paired & (shared_start == 4))
     def _():
         add_shared(3)
 
@@ -368,6 +397,7 @@
                 for block in NEXT[half]:
                     give_back[at, block - 3] = total_of(half, at, block).astype(jnp.bfloat16)
                     back_copy(block - 3, at).start()
+            for at in (1 - half, half):
                 for index in range(3):
                     total = total_of(half, at, index)
                     if at == half:
@@ -429,8 +459,10 @@
 
 
 def body(blocks, eps_occ, eps_vir, pairs):
-    eps = jnp.broadcast_to(eps_occ.reshape(3, ORB, 1), (3, ORB, 128))
-    vir = jnp.pad(eps_vir, (0, PAD - VIRT)).reshape(1, PAD)
+    eps = eps_occ.reshape(1, 3 * ORB)
+    vir = eps_vir.reshape(1, VIRT)
+    slots = pairs.T
+    anywhere = pl.BlockSpec(memory_space=pl.ANY)
     vmem = pl.BlockSpec(memory_space=pltpu.VMEM)
     bf16, f32 = jnp.bfloat16, jnp.float32
     dma = pltpu.SemaphoreType.DMA
@@ -438,12 +470,18 @@
     return pl.pallas_call(
         kernel,
         out_shape=jax.ShapeDtypeStruct(blocks.shape, f32),
-        in_specs=[vmem] * 4,
+        in_specs=[anywhere] * 4,
         out_specs=vmem,
         scratch_shapes=[
             pltpu.VMEM((3,) + slab, bf16),
+            pltpu.VMEM((2, 1, 3 * ORB), f32),
+            pltpu.VMEM((1, VIRT), f32),
+            pltpu.VMEM(slots.shape, jnp.int32),
+            dma((4,)),
+            pltpu.VMEM((3,) + slab, bf16),
             pltpu.VMEM((2, 3) + slab, bf16),
-            pltpu.VMEM((6, ORB, 128), f32),
+            pltpu.VMEM((2, ORB, PAD), f32),
+            pltpu.VMEM((1, PAD), f32),
             pltpu.VMEM((COLS,) + slab, bf16),
             pltpu.VMEM((COLS,) + slab, bf16),
             pltpu.VMEM((2, FULL, WIDE), bf16),
@@ -471,7 +509,7 @@
             collective_id=0, has_side_effects=True, vmem_limit_bytes=48 * 1024 * 1024
         ),
         cost_estimate=pl.CostEstimate(flops=6 * FULL**3, bytes_accessed=4 * 1024 * 1024, transcendentals=0),
-    )(blocks, eps, vir, pairs)
+    )(blocks, eps, vir, slots)
 
 
 def solution(mesh):

time: 92.9 us -> 82.9 us (0.89)
  the two profiles are of different devices: /device:TPU:10 before, /device:TPU:1 now
where the time goes in v3:
time: 82.9 us; the launch traced here: 82.1 us
  Pallas kernels  79.6 us (96%)
  local copies, waits for them, and re-layouts  2.48 us (3%)
    pallas_call x1, Pallas kernels, body(): pl.pallas_call(kernel, out_shape=jax.ShapeDtypeStruct(blocks.shape, f32),...  79.6 us
    unnamed x9, local copies, waits for them, and re-layouts  2.48 us

profile of v3, /device:TPU:1, one launch (start us, length us, event | category | flops | bytes accessed | tf_op | source)
XLA Modules:
  0.0 82.1 jit_solution(6897513522089191238)
XLA Ops:
  0.0 0.0 copy-start.2
  0.0 0.0 copy-start.1
  0.0 0.0 copy-start.3
  0.0 0.7 copy-done.2
  0.7 0.0 copy-done.1
  0.7 0.0 copy-done.3
  0.7 0.0 copy-start
  0.7 1.0 %copy-done = bf16[3,56,896]{2,1,0:T(8,128)(2,1)S(1)} copy-done((bf16[3,56,896]{2,1,0:T(8,128)(2,1)S(1)}, bf16[3,56,896]{2,1,0:T(8,128)(2,1)}, u32[]{:S(2)}) %copy-start) | copy-done | bytes 301080
  1.7 79.6 %shard_map.46 = f32[3,56,896]{2,1,0:T(8,128)S(1)} custom-call(bf16[3,56,896]{2,1,0:T(8,128)(2,1)S(1)} %copy-done, f32[1,12]{1,0:T(1,128)S(1)} %bitcast.5, f32[1,224]{1,0:T(1,128)S(1)} %bitcast.3, s32[2,32]{1,0:T(2,128)S(1)} %bitcast.4), custom_call_target="tpu_custom_call" | custom-call | flops 6442450944 | bytes 4194304 | tf_op jit(solution)/shard_map/pallas_call | solution.py:470
  81.3 0.8 %copy.6 = f32[3,56,896]{2,1,0:T(8,128)} copy(f32[3,56,896]{2,1,0:T(8,128)S(1)} %shard_map.46) | data formatting | bytes 1204224
Async XLA Ops:
  0.0 0.7 copy-start.2
  0.0 0.7 copy-start.1
  0.0 0.7 copy-start.3
  0.7 1.0 %copy-start = (bf16[3,56,896]{2,1,0:T(8,128)(2,1)S(1)}, bf16[3,56,896]{2,1,0:T(8,128)(2,1)}, u32[]{:S(2)}) copy-start(bf16[3,56,896]{2,1,0:T(8,128)(2,1)} %blocks_in.1) | copy-start | bytes 903172
